TPU v7x, 32 devices: a whole 2x2x4 slice. The times are simulated.
32 devices in a mesh: video: 2 (over y), rows: 4 (over z), cols: 4 (over x, core).
Axes of the slice: x: 2, y: 2, z: 4, core: 2. Of those that a mesh axis runs over, the one named last changes fastest.
Arguments:
- frame_in: bfloat16 [64, 80, 512], P(('video', 'rows'), 'cols'), parts along dimension 0, may hold values from -6 to 6
- norm_gain: float32 [512], replicated, may hold values from 0.5 to 1.5
- w_query: bfloat16 [512, 512], replicated, may hold values from -2 to 2
- w_key: bfloat16 [512, 512], replicated, may hold values from -0.125 to 0.125
- w_value: bfloat16 [512, 512], replicated, may hold values from -0.25 to 0.25
- w_out: bfloat16 [512, 512], replicated, may hold values from -0.25 to 0.25
- conv_gain: float32 [512], replicated, may hold values from 0.5 to 1.5
- conv_cache: bfloat16 [2, 64, 80, 512], P(None, ('video', 'rows'), 'cols'), parts along dimension 1, may hold values from -6 to 6
- w_conv: bfloat16 [3, 3, 3, 512, 256], replicated, may hold values from -0.0546875 to 0.0546875
- conv_bias: float32 [256], replicated, may hold values from -0.5 to 0.5
Outputs:
- hidden: bfloat16 [64, 80, 512], P(('video', 'rows'), 'cols'), parts along dimension 0
- mixed_out: bfloat16 [64, 80, 256], P(('video', 'rows'), 'cols'), parts along dimension 0
There are 2 independent parts, one for each index of `video`. A program takes and returns all parts, laid end to end along the dimension named above; an argument that names none is the same for every part. Nothing has to cross between parts.
All inputs are finite; a program needn't handle non-finite values.
Results may differ from a plain program's by a relative error of at most 0.012.
Values may be sent and summed in bfloat16 or wider, within the bound.
A program may use at most 128 MiB of HBM per device.

v0:
```python
import math

import jax
import jax.numpy as jnp
from jax import lax
from jax.sharding import PartitionSpec as P


def padded_2(value, sides, width):
    for axis, dim in sides:
        size, length = (lax.axis_size(axis), value.shape[dim])
        up = [(i, (i + 1) % size) for i in range(size - 1)]
        down = [(j, i) for i, j in up]
        last = lax.slice_in_dim(value, length - width, length, axis=dim)
        first = lax.slice_in_dim(value, 0, width, axis=dim)
        before = lax.ppermute(last, axis, up)
        after = lax.ppermute(first, axis, down)
        value = jnp.concatenate([before, value, after], axis=dim)
    return value


def rms_scaled(values, gain):
    mean_sq = jnp.mean(values * values, axis=-1, keepdims=True)
    return values * lax.rsqrt(mean_sq + 1e-06) * gain


def fold_block(running_state, query_keys, block_rows):
    running, total_sum, accumulated = running_state
    scores = lax.dot_general(
        query_keys, block_rows, (((1,), (1,)), ((), ())), preferred_element_type=jnp.float32
    )
    new_max = jnp.maximum(running, jnp.max(scores, axis=1))
    weights = jnp.exp(scores - new_max[:, None])
    total_sum = jnp.sum(weights, axis=1)
    accumulated = jnp.dot(
        weights.astype(jnp.bfloat16), block_rows, preferred_element_type=jnp.float32
    )
    return (new_max, total_sum, accumulated)


def start_for(query_count, channels):
    return (
        jnp.full((query_count,), -1e30, jnp.float32),
        jnp.zeros((query_count,), jnp.float32),
        jnp.zeros((query_count, channels), jnp.float32),
    )


def body(
    frame_in, norm_gain, w_query, w_key, w_value, w_out, conv_gain, conv_cache, w_conv, conv_bias
):
    tile_rows, tile_cols, channels = frame_in.shape
    out_channels = w_conv.shape[4]
    count = tile_rows * tile_cols
    cache_padded = padded_2(conv_cache, (("rows", 1), ("cols", 2)), 1)
    tokens = frame_in.astype(jnp.float32).reshape(count, channels)
    normed = rms_scaled(tokens, norm_gain).astype(jnp.bfloat16)
    query_rows = (
        jnp.dot(normed, w_query, preferred_element_type=jnp.float32) * (1.0 / math.sqrt(channels))
    ).astype(jnp.bfloat16)
    query_keys = jnp.dot(query_rows, w_key.T, preferred_element_type=jnp.float32).astype(
        jnp.bfloat16
    )
    final_state = fold_block(
        start_for(count, channels),
        query_keys,
        lax.all_gather(normed, ("rows", "cols"), axis=0, tiled=True),
    )
    pooled = (final_state[2] / final_state[1][:, None]).astype(jnp.bfloat16)
    attended = jnp.dot(pooled, w_value, preferred_element_type=jnp.float32).astype(jnp.bfloat16)
    hidden = (tokens + jnp.dot(attended, w_out, preferred_element_type=jnp.float32)).astype(
        jnp.bfloat16
    )
    conv_input = jax.nn.silu(rms_scaled(hidden.astype(jnp.float32), conv_gain)).astype(jnp.bfloat16)
    conv_input = conv_input.reshape(1, tile_rows, tile_cols, channels)
    frame_padded = padded_2(conv_input, (("rows", 1), ("cols", 2)), 1)
    padded = jnp.concatenate([cache_padded, frame_padded], axis=0)
    windows = [
        padded[time_off, row_off : row_off + tile_rows, col_off : col_off + tile_cols, :]
        for time_off in range(3)
        for row_off in range(3)
        for col_off in range(3)
    ]
    patches = jnp.concatenate(windows, axis=-1).reshape(count, 27 * channels)
    kernel_rows = w_conv.reshape(27 * channels, out_channels)
    result_sum = hidden[:, :out_channels].astype(jnp.float32) + conv_bias
    result_sum = result_sum + jnp.dot(patches, kernel_rows, preferred_element_type=jnp.float32)
    hidden_out = hidden.reshape(tile_rows, tile_cols, channels)
    mixed_out = result_sum.astype(jnp.bfloat16).reshape(tile_rows, tile_cols, out_channels)
    return (hidden_out, mixed_out)


def solution(mesh):
    in_specs = (
        P(("video", "rows"), "cols", None),
        P(),
        P(),
        P(),
        P(),
        P(),
        P(),
        P(None, ("video", "rows"), "cols", None),
        P(),
        P(),
    )
    out_specs = (P(("video", "rows"), "cols", None), P(("video", "rows"), "cols", None))
    return jax.shard_map(body, mesh=mesh, in_specs=in_specs, out_specs=out_specs, check_vma=False)
```

profile of v0, /device:TPU:1, one launch (start us, length us, event | category | flops | bytes accessed | tf_op | source)
XLA Modules:
  0.0 101.2 jit_solution(12430634139479733988)
XLA Ops:
  7.2 1.1 %copy.97 = f32[8,20,512]{2,1,0:T(8,128)S(1)} copy(bf16[8,20,512]{2,0,1:T(8,128)(2,1)} %param.10) | data formatting | bytes 491520 | tf_op jit(solution)/shard_map/convert_element_type | solution.py:56
  8.3 1.0 %multiply_reduce_fusion = f32[8,20]{0,1:T(8,128)S(1)} fusion(bf16[8,20,512]{2,0,1:T(8,128)(2,1)} %param.10), kind=kLoop, calls=%fused_computation.32 | loop fusion | flops 245600 | bytes 164480 | tf_op jit(solution)/shard_map/reduce_sum | solution.py:23
  9.6 1.5 %multiply_convert_fusion = bf16[160,512]{1,0:T(8,128)(2,1)} fusion(f32[160,512]{1,0:T(8,128)S(1)} %reshape.106, f32[512]{0:T(512)} %param.11, f32[160]{0:T(256)S(1)} %rsqrt.20), kind=kLoop, calls=%fused_computation.31 | loop fusion | flops 245760 | bytes 494208 | tf_op jit(solution)/shard_map/convert_element_type | solution.py:57
  11.0 1.2 %fusion.28 = (bf16[2,1,20,512]{3,1,2,0:T(2,128)(2,1)S(1)}, bf16[2,1,20,512]{3,1,2,0:T(2,128)(2,1)S(1)}) fusion(bf16[2,8,20,512]{3,1,2,0:T(8,128)(2,1)} %param.17), kind=kLoop, calls=%fused_computation.90 | loop fusion | bytes 163840 | tf_op jit(solution)/shard_map/slice | solution.py:14
  12.2 1.3 %collective-permute-start.1 = (bf16[2,1,20,512]{3,1,2,0:T(2,128)(2,1)S(1)}, bf16[2,1,20,512]{3,1,2,0:T(2,128)(2,1)S(1)}, u32[]{:S(2)}, u32[]{:S(2)}) collective-permute-start(bf16[2,1,20,512]{3,1,2,0:T(2,128)(2,1)S(1)} %get-tuple-element.37), channel_id=1, source_target_pairs={{4,0},{8,4},{12,8},{5,1},{9,5},{13,9},{6,2},{10,6},{14,10},{7,3},{... | collective-permute-start | bytes 122888 | tf_op jit(solution)/shard_map/ppermute | solution.py:17
  13.5 4.7 %collective-permute-start = (bf16[2,1,20,512]{3,1,2,0:T(2,128)(2,1)S(1)}, bf16[2,1,20,512]{3,1,2,0:T(2,128)(2,1)S(1)}, u32[]{:S(2)}, u32[]{:S(2)}) collective-permute-start(bf16[2,1,20,512]{3,1,2,0:T(2,128)(2,1)S(1)} %get-tuple-element.36), channel_id=1, source_target_pairs={{0,4},{4,8},{8,12},{1,5},{5,9},{9,13},{2,6},{6,10},{10,14},{3,7},{... | collective-permute-start | bytes 122888 | tf_op jit(solution)/shard_map/ppermute | solution.py:16
  18.2 1.4 %fusion.2 = bf16[160,512]{1,0:T(8,128)(2,1)S(1)} fusion(bf16[160,512]{1,0:T(8,128)(2,1)} %multiply_convert_fusion, bf16[512,512]{1,0:T(8,128)(2,1)} %param.12), kind=kOutput, calls=%fused_computation.6 | convolution fusion | flops 84049920 | bytes 851968 | tf_op jit(solution)/shard_map/dot_general | solution.py:59
  19.6 1.0 constant_dynamic-update-slice_fusion.1
  20.6 0.8 pad_maximum_fusion.7
  21.4 2.9 %collective-permute-start.3 = (bf16[2,10,1,512]{3,1,2,0:T(8,128)(2,1)S(1)}, bf16[2,10,1,512]{3,1,2,0:T(8,128)(2,1)S(1)}, u32[]{:S(2)}, u32[]{:S(2)}) collective-permute-start(bf16[2,10,1,512]{3,1,2,0:T(8,128)(2,1)S(1)} %get-tuple-element.28), channel_id=1, source_target_pairs={{1,0},{2,1},{3,2},{5,4},{6,5},{7,6},{9,8},{10,9},{11,10},{13,12},{... | collective-permute-start | bytes 61448 | tf_op jit(solution)/shard_map/ppermute | solution.py:17
  24.3 3.5 %collective-permute-start.2 = (bf16[2,10,1,512]{3,1,2,0:T(8,128)(2,1)S(1)}, bf16[2,10,1,512]{3,1,2,0:T(8,128)(2,1)S(1)}, u32[]{:S(2)}, u32[]{:S(2)}) collective-permute-start(bf16[2,10,1,512]{3,1,2,0:T(8,128)(2,1)S(1)} %get-tuple-element.29), channel_id=1, source_target_pairs={{0,1},{1,2},{2,3},{4,5},{5,6},{6,7},{8,9},{9,10},{10,11},{12,13},{... | collective-permute-start | bytes 61448 | tf_op jit(solution)/shard_map/ppermute | solution.py:16
  27.8 0.1 constant_dynamic-update-slice_fusion
  27.9 0.2 fusion.27
  28.8 0.6 pad_maximum_fusion
  29.5 1.2 %fusion.24 = (bf16[1,8,20,512]{3,1,2,0:T(8,128)(2,1)}, bf16[1,8,20,512]{3,1,2,0:T(8,128)(2,1)S(1)}, bf16[1,8,20,512]{3,1,2,0:T(8,128)(2,1)S(1)}, bf16[1,8,20,512...) fusion(bf16[2,10,21,512]{3,1,2,0:T(8,128)(2,1)S(1)} %get-tuple-, ...), kind=kLoop, calls=%fused_computation.86 | loop fusion | bytes 3932160 | tf_op jit(solution)/shard_map/slice | solution.py:79
  30.7 0.7 concatenate.106
  31.4 1.0 copy.101
  32.4 1.0 copy.102
  33.4 0.7 concatenate.111
  34.1 1.0 copy.104
  35.2 0.7 concatenate.114
  36.4 1.0 copy.114
  37.4 1.6 %constant_dynamic-update-slice_fusion.31 = bf16[160,13824]{1,0:T(8,128)(2,1)} fusion(bf16[160,512]{1,0:T(8,128)(2,1)} %concatenate.106), kind=kLoop, calls=%fused_computation.79 | loop fusion | bytes 327680
  39.0 0.7 constant_dynamic-update-slice_fusion.30
  39.7 0.7 constant_dynamic-update-slice_fusion.29
  40.4 1.6 %constant_dynamic-update-slice_fusion.28 = bf16[160,13824]{1,0:T(8,128)(2,1)} fusion(bf16[160,13824]{1,0:T(8,128)(2,1)} %constant_dynamic-update-slice_fusion.29, bf16[160,512]{1,0:T(8,128)(2,1)} %concatenate.111), kind=kLoop, calls=%fused_computation.76 | loop fusion | bytes 327680
  42.0 0.7 constant_dynamic-update-slice_fusion.27
  42.7 0.7 constant_dynamic-update-slice_fusion.26
  43.4 1.6 %constant_dynamic-update-slice_fusion.25 = bf16[160,13824]{1,0:T(8,128)(2,1)} fusion(bf16[160,13824]{1,0:T(8,128)(2,1)} %constant_dynamic-update-slice_fusion.26, bf16[160,512]{1,0:T(8,128)(2,1)} %concatenate.114), kind=kLoop, calls=%fused_computation.73 | loop fusion | bytes 327680
  45.0 0.7 constant_dynamic-update-slice_fusion.24
  45.7 0.7 constant_dynamic-update-slice_fusion.23
  46.5 0.7 constant_dynamic-update-slice_fusion.22
  47.2 0.7 constant_dynamic-update-slice_fusion.21
  47.9 0.7 constant_dynamic-update-slice_fusion.20
  48.5 0.7 constant_dynamic-update-slice_fusion.19
  49.2 0.7 constant_dynamic-update-slice_fusion.18
  49.9 0.7 constant_dynamic-update-slice_fusion.17
  50.6 0.7 constant_dynamic-update-slice_fusion.16
  51.3 5.6 %all-gather.2.cloned.1.call-done = bf16[2560,512]{1,0:T(8,128)(2,1)} async-done(((bf16[160,512]{1,0:T(8,128)(2,1)}), bf16[2560,512]{1,0:T(8,128)(2,1)}) %all-gather.2.cloned.1.call-update) | async-done | bytes 2621456 | tf_op jit(solution)/shard_map/all_gather | solution.py:67
  56.9 3.1 %fusion.31 = (f32[160]{0:T(256)S(1)}, f32[160,2560]{1,0:T(8,128)S(1)}) fusion(bf16[2560,512]{1,0:T(8,128)(2,1)} %all-gather.2.cloned.1.call-done, bf16[160,512]{1,0:T(8,128)(2,1)S(1)} %fusion.2, bf16[512,512]{1,0:T(8,128)(2,1)S(1)} %copy-done), kind=kOutput, calls=%fused_computation.93 | convolution fusion | flops 503807840 | bytes 4948608 | tf_op jit(solution)/shard_map/dot_general | solution.py:29
  60.0 0.4 fusion
  60.4 3.3 %convolution_convert_fusion = bf16[160,512]{1,0:T(8,128)(2,1)} fusion(bf16[512,512]{1,0:T(8,128)(2,1)} %param.14, bf16[2560,512]{1,0:T(8,128)(2,1)} %all-gather.2.cloned.1.call-done, f32[160,2560]{1,0:T(8,128)S(1)} %get-tuple-element.55, f32[160]{0:T(256)S(1)} %broadcast_maximum_fusion, f32[160]{0:T(256)S(1)} %fusion), kind=kOutput, calls=%fused_computation.8 | convolution fusion | flops 504381440 | bytes 4949248 | tf_op jit(solution)/shard_map/dot_general | solution.py:70
  63.8 1.3 %fusion.11 = (f32[160]{0:T(256)S(1)}, bf16[160,512]{1,0:T(8,128)(2,1)S(1)}) fusion(f32[160,512]{1,0:T(8,128)S(1)} %reshape.106, bf16[160,512]{1,0:T(8,128)(2,1)} %convolution_convert_fusion, bf16[512,512]{1,0:T(8,128)(2,1)S(1)} %copy-done.3), kind=kOutput, calls=%fused_computation.23 | convolution fusion | flops 84295520 | bytes 1180288 | tf_op jit(solution)/shard_map/dot_general | solution.py:71
  65.0 0.2 fusion.18
  65.3 2.9 %collective-permute-start.4 = (bf16[1,1,20,512]{3,2,1,0:T(8,128)(2,1)S(1)}, bf16[1,1,20,512]{3,2,1,0:T(8,128)(2,1)S(1)}, u32[]{:S(2)}, u32[]{:S(2)}) collective-permute-start(bf16[1,1,20,512]{3,2,1,0:T(8,128)(2,1)S(1)} %get-tuple-element.53), channel_id=1, source_target_pairs={{0,4},{4,8},{8,12},{1,5},{5,9},{9,13},{2,6},{6,10},{10,14},{3,7},{... | collective-permute-start | bytes 61448 | tf_op jit(solution)/shard_map/ppermute | solution.py:16
  68.2 0.7 constant_dynamic-update-slice_fusion.15
  69.0 1.3 %collective-permute-start.5 = (bf16[1,1,20,512]{3,2,1,0:T(8,128)(2,1)S(1)}, bf16[1,1,20,512]{3,2,1,0:T(8,128)(2,1)S(1)}, u32[]{:S(2)}, u32[]{:S(2)}) collective-permute-start(bf16[1,1,20,512]{3,2,1,0:T(8,128)(2,1)S(1)} %get-tuple-element.52), channel_id=1, source_target_pairs={{4,0},{8,4},{12,8},{5,1},{9,5},{13,9},{6,2},{10,6},{14,10},{7,3},{... | collective-permute-start | bytes 61448 | tf_op jit(solution)/shard_map/ppermute | solution.py:17
  70.3 3.2 %collective-permute-done.5 = bf16[1,1,20,512]{3,2,1,0:T(8,128)(2,1)S(1)} collective-permute-done((bf16[1,1,20,512]{3,2,1,0:T(8,128)(2,1)S(1)}, bf16[1,1,20,512]{3,2,1,0:T(8,128)(2,1)S(1)}, u32[]{:S(2)}, u32[]{:S(2)}) %collective-permute-start.5) | collective-permute-done | bytes 20512 | tf_op jit(solution)/shard_map/ppermute | solution.py:17
  73.7 3.6 %collective-permute-start.7 = (bf16[1,10,1,512]{3,2,1,0:T(2,128)(2,1)S(1)}, bf16[1,10,1,512]{3,2,1,0:T(2,128)(2,1)S(1)}, u32[]{:S(2)}, u32[]{:S(2)}) collective-permute-start(bf16[1,10,1,512]{3,2,1,0:T(2,128)(2,1)S(1)} %get-tuple-element.47), channel_id=1, source_target_pairs={{1,0},{2,1},{3,2},{5,4},{6,5},{7,6},{9,8},{10,9},{11,10},{13,12},{... | collective-permute-start | bytes 30728 | tf_op jit(solution)/shard_map/ppermute | solution.py:17
  77.3 2.1 %collective-permute-start.6 = (bf16[1,10,1,512]{3,2,1,0:T(2,128)(2,1)S(1)}, bf16[1,10,1,512]{3,2,1,0:T(2,128)(2,1)S(1)}, u32[]{:S(2)}, u32[]{:S(2)}) collective-permute-start(bf16[1,10,1,512]{3,2,1,0:T(2,128)(2,1)S(1)} %get-tuple-element.48), channel_id=1, source_target_pairs={{0,1},{1,2},{2,3},{4,5},{5,6},{6,7},{8,9},{9,10},{10,11},{12,13},{... | collective-permute-start | bytes 30728 | tf_op jit(solution)/shard_map/ppermute | solution.py:16
  79.4 0.7 constant_dynamic-update-slice_fusion.14
  80.1 0.7 copy.117
  80.9 0.3 pad_maximum_fusion.1
  81.4 0.7 constant_dynamic-update-slice_fusion.13
  82.1 0.7 constant_dynamic-update-slice_fusion.12
  82.8 0.7 constant_dynamic-update-slice_fusion.11
  83.5 0.7 constant_dynamic-update-slice_fusion.10
  84.2 0.9 constant_dynamic-update-slice_fusion.9
  85.2 0.7 constant_dynamic-update-slice_fusion.8
  85.9 0.7 constant_dynamic-update-slice_fusion.7
  86.5 0.7 constant_dynamic-update-slice_fusion.6
  87.2 0.7 constant_dynamic-update-slice_fusion.5
  87.9 5.7 %fusion.6 = bf16[160,256]{1,0:T(8,128)(2,1)S(1)} fusion(bf16[160,13824]{1,0:T(8,128)(2,1)} %constant_dynamic-update-slice_fusion.5, bf16[13824,256]{1,0:T(8,128)(2,1)} %bitcast.12, bf16[160,512]{1,0:T(8,128)(2,1)S(1)} %get-tuple-element.57, f32[256]{0:T(256)S(1)} %copy-done.5), kind=kOutput, calls=%fused_computation.13 | convolution fusion | flops 1132625920 | bytes 11666432 | tf_op jit(solution)/shard_map/dot_general | solution.py:87
  93.7 0.7 copy.118
  (73 shorter events, 2.2 us)
Async XLA Ops:
  7.2 49.8 %copy-start = (bf16[512,512]{1,0:T(8,128)(2,1)S(1)}, bf16[512,512]{1,0:T(8,128)(2,1)}, u32[]{:S(2)}) copy-start(bf16[512,512]{1,0:T(8,128)(2,1)} %param.13) | copy-start | bytes 1572868
  7.2 20.7 %copy-start.1 = (bf16[2,8,20,512]{3,1,2,0:T(8,128)(2,1)S(1)}, bf16[2,8,20,512]{3,1,2,0:T(8,128)(2,1)}, u32[]{:S(2)}) copy-start(bf16[2,8,20,512]{3,1,2,0:T(8,128)(2,1)} %param.17) | copy-start | bytes 983044
  7.2 49.7 %all-gather.2.cloned.1.call-start = ((), (), s32[]{:S(2)}) async-start(), calls=%async_computation | async-start | bytes 2785280 | tf_op jit(solution)/shard_map/all_gather | solution.py:67
  12.2 8.4 %collective-permute-start.1 = (bf16[2,1,20,512]{3,1,2,0:T(2,128)(2,1)S(1)}, bf16[2,1,20,512]{3,1,2,0:T(2,128)(2,1)S(1)}, u32[]{:S(2)}, u32[]{:S(2)}) collective-permute-start(bf16[2,1,20,512]{3,1,2,0:T(2,128)(2,1)S(1)} %get-tuple-element.37), channel_id=1, source_target_pairs={{4,0},{8,4},{12,8},{5,1},{9,5},{13,9},{6,2},{10,6},{14,10},{7,3},{... | collective-permute-start | bytes 122888 | tf_op jit(solution)/shard_map/ppermute | solution.py:17
  13.5 7.1 %collective-permute-start = (bf16[2,1,20,512]{3,1,2,0:T(2,128)(2,1)S(1)}, bf16[2,1,20,512]{3,1,2,0:T(2,128)(2,1)S(1)}, u32[]{:S(2)}, u32[]{:S(2)}) collective-permute-start(bf16[2,1,20,512]{3,1,2,0:T(2,128)(2,1)S(1)} %get-tuple-element.36), channel_id=1, source_target_pairs={{0,4},{4,8},{8,12},{1,5},{5,9},{9,13},{2,6},{6,10},{10,14},{3,7},{... | collective-permute-start | bytes 122888 | tf_op jit(solution)/shard_map/ppermute | solution.py:16
  21.4 7.4 %collective-permute-start.3 = (bf16[2,10,1,512]{3,1,2,0:T(8,128)(2,1)S(1)}, bf16[2,10,1,512]{3,1,2,0:T(8,128)(2,1)S(1)}, u32[]{:S(2)}, u32[]{:S(2)}) collective-permute-start(bf16[2,10,1,512]{3,1,2,0:T(8,128)(2,1)S(1)} %get-tuple-element.28), channel_id=1, source_target_pairs={{1,0},{2,1},{3,2},{5,4},{6,5},{7,6},{9,8},{10,9},{11,10},{13,12},{... | collective-permute-start | bytes 61448 | tf_op jit(solution)/shard_map/ppermute | solution.py:17
  24.3 4.5 %collective-permute-start.2 = (bf16[2,10,1,512]{3,1,2,0:T(8,128)(2,1)S(1)}, bf16[2,10,1,512]{3,1,2,0:T(8,128)(2,1)S(1)}, u32[]{:S(2)}, u32[]{:S(2)}) collective-permute-start(bf16[2,10,1,512]{3,1,2,0:T(8,128)(2,1)S(1)} %get-tuple-element.29), channel_id=1, source_target_pairs={{0,1},{1,2},{2,3},{4,5},{5,6},{6,7},{8,9},{9,10},{10,11},{12,13},{... | collective-permute-start | bytes 61448 | tf_op jit(solution)/shard_map/ppermute | solution.py:16
  60.0 3.8 %copy-start.3 = (bf16[512,512]{1,0:T(8,128)(2,1)S(1)}, bf16[512,512]{1,0:T(8,128)(2,1)}, u32[]{:S(2)}) copy-start(bf16[512,512]{1,0:T(8,128)(2,1)} %param.15) | copy-start | bytes 1572868
  60.0 5.0 %copy-start.4 = (f32[512]{0:T(512)S(1)}, f32[512]{0:T(512)}, u32[]{:S(2)}) copy-start(f32[512]{0:T(512)} %param.16) | copy-start | bytes 6148
  60.0 8.9 %copy-start.2 = (bf16[1,8,20,512]{3,1,2,0:T(8,128)(2,1)S(1)}, bf16[1,8,20,512]{3,1,2,0:T(8,128)(2,1)}, u32[]{:S(2)}) copy-start(bf16[1,8,20,512]{3,1,2,0:T(8,128)(2,1)} %get-tuple-element.12) | copy-start | bytes 491524
  65.3 5.0 %collective-permute-start.4 = (bf16[1,1,20,512]{3,2,1,0:T(8,128)(2,1)S(1)}, bf16[1,1,20,512]{3,2,1,0:T(8,128)(2,1)S(1)}, u32[]{:S(2)}, u32[]{:S(2)}) collective-permute-start(bf16[1,1,20,512]{3,2,1,0:T(8,128)(2,1)S(1)} %get-tuple-element.53), channel_id=1, source_target_pairs={{0,4},{4,8},{8,12},{1,5},{5,9},{9,13},{2,6},{6,10},{10,14},{3,7},{... | collective-permute-start | bytes 61448 | tf_op jit(solution)/shard_map/ppermute | solution.py:16
  69.0 4.6 %collective-permute-start.5 = (bf16[1,1,20,512]{3,2,1,0:T(8,128)(2,1)S(1)}, bf16[1,1,20,512]{3,2,1,0:T(8,128)(2,1)S(1)}, u32[]{:S(2)}, u32[]{:S(2)}) collective-permute-start(bf16[1,1,20,512]{3,2,1,0:T(8,128)(2,1)S(1)} %get-tuple-element.52), channel_id=1, source_target_pairs={{4,0},{8,4},{12,8},{5,1},{9,5},{13,9},{6,2},{10,6},{14,10},{7,3},{... | collective-permute-start | bytes 61448 | tf_op jit(solution)/shard_map/ppermute | solution.py:17
  73.6 14.3 %copy-start.5 = (f32[256]{0:T(256)S(1)}, f32[256]{0:T(256)}, u32[]{:S(2)}) copy-start(f32[256]{0:T(256)} %param.19) | copy-start | bytes 3076
  73.7 7.2 %collective-permute-start.7 = (bf16[1,10,1,512]{3,2,1,0:T(2,128)(2,1)S(1)}, bf16[1,10,1,512]{3,2,1,0:T(2,128)(2,1)S(1)}, u32[]{:S(2)}, u32[]{:S(2)}) collective-permute-start(bf16[1,10,1,512]{3,2,1,0:T(2,128)(2,1)S(1)} %get-tuple-element.47), channel_id=1, source_target_pairs={{1,0},{2,1},{3,2},{5,4},{6,5},{7,6},{9,8},{10,9},{11,10},{13,12},{... | collective-permute-start | bytes 30728 | tf_op jit(solution)/shard_map/ppermute | solution.py:17
  77.3 3.6 %collective-permute-start.6 = (bf16[1,10,1,512]{3,2,1,0:T(2,128)(2,1)S(1)}, bf16[1,10,1,512]{3,2,1,0:T(2,128)(2,1)S(1)}, u32[]{:S(2)}, u32[]{:S(2)}) collective-permute-start(bf16[1,10,1,512]{3,2,1,0:T(2,128)(2,1)S(1)} %get-tuple-element.48), channel_id=1, source_target_pairs={{0,1},{1,2},{2,3},{4,5},{5,6},{6,7},{8,9},{9,10},{10,11},{12,13},{... | collective-permute-start | bytes 30728 | tf_op jit(solution)/shard_map/ppermute | solution.py:16
Sparse Core Ops, SparseCore 0:
  11.1 45.7 all-gather.1
where the time goes:
time: 102 us; the launch traced here: 101 us
  local copies, waits for them, and re-layouts  34.8 us (34%)
  starting transfers between devices  22.2 us (22%)
  matrix products  14.7 us (14%)
  between operations  14.7 us (14%)
  waiting for transfers between devices  8.92 us (9%)
  other arithmetic  5.83 us (6%)
    unnamed x41, local copies, waits for them, and re-layouts  22.5 us
    ppermute x4, starting transfers between devices, padded_2(): before = lax.ppermute(last, axis, up)  13.1 us
    ppermute x4, starting transfers between devices, padded_2(): after = lax.ppermute(first, axis, down)  9.05 us
    slice x20, local copies, waits for them, and re-layouts, body(): padded[time_off, row_off:row_off + tile_rows, col_off:col_off + tile_cols...  5.92 us
    dot_general x1, matrix products, body(): jnp.dot(patches, kernel_rows, preferred_element_type=jnp.float32)  5.69 us
    all_gather x1, waiting for transfers between devices, body(): lax.all_gather(normed, ('rows', 'cols'), axis=0, tiled=True)  5.64 us
    concatenate x27, local copies, waits for them, and re-layouts, body(): patches = jnp.concatenate(windows, axis=-1).reshape(count, 27 * channels)  3.61 us
    dot_general x1, matrix products, body(): jnp.dot(pooled, w_value, preferred_element_type=jnp.float32)  3.34 us
  transfers between devices with their start and end apart: 9, of which 2 were waited for; matrix products, arithmetic and copies ran while one was open for 30% of the time, Pallas kernels for 0%

commit v1 on v0

v1 whole, which is shorter than its diff:
```python
import functools
import math

import jax
import jax.numpy as jnp
from jax import lax
from jax.experimental import pallas as pl
from jax.experimental.pallas import tpu as pltpu
from jax.sharding import PartitionSpec as P

MESH = pl.DeviceIdType.MESH
F32 = jnp.float32
BF16 = jnp.bfloat16
PITCH = 32


def rms_scaled(values, gain):
    mean_sq = jnp.mean(values * values, axis=-1, keepdims=True)
    return values * lax.rsqrt(mean_sq + 1e-06) * gain


def kernel(
    rows, cols, frame_ref, ngain_ref, wq_hbm, wk_hbm, wv_hbm, wo_hbm, cgain_ref, cache_hbm, wc_hbm, bias_ref,
    hidden_ref, mixed_ref,
    wq, wk, wv, wo, wc, cache, kv, tok, qk, acc, peak, total, xp, col_out, col_in, sums,
    load_sem, z_send, x_send, d_send, recv_sem, halo_send, halo_recv,
):
    tile_rows, tile_cols, channels = frame_ref.shape
    out_channels = wc.shape[-1]
    count = tile_rows * tile_cols
    v, r, c = lax.axis_index("video"), lax.axis_index("rows"), lax.axis_index("cols")
    nx = cols // 2
    x, lane = c // 2, c % 2
    sibling = x * 2 + 1 - lane
    me = r * cols + c

    loads = [
        pltpu.make_async_copy(src, dst, load_sem.at[n])
        for n, (src, dst) in enumerate(
            [(cache_hbm, cache), (wq_hbm, wq), (wk_hbm, wk), (wc_hbm, wc), (wv_hbm, wv), (wo_hbm, wo)]
        )
    ]
    for load in loads:
        load.start()

    barrier = pltpu.get_barrier_semaphore()

    @pl.loop(0, rows * cols)
    def _(d):
        @pl.when(d != me)
        def _():
            pl.semaphore_signal(barrier, inc=1, device_id=(v, d // cols, d % cols), device_id_type=MESH)

    for q in range(tile_rows):
        tok[pl.ds(q * tile_cols, tile_cols), :] = frame_ref[q].astype(F32)
    normed = rms_scaled(tok[...], ngain_ref[...]).astype(BF16)
    kv[me] = normed

    pl.semaphore_wait(barrier, rows * cols - 1)

    def push(slot, row, col, send_sem):
        return pltpu.make_async_remote_copy(
            src_ref=kv.at[slot], dst_ref=kv.at[slot], send_sem=send_sem, recv_sem=recv_sem.at[slot],
            device_id=(v, row, col), device_id_type=MESH,
        )

    def z_copy(k):
        return push(me, (r + rows - k) % rows, c, z_send.at[k])

    def x_copy(k, d):
        slot = ((r + k) % rows) * cols + c
        return push(slot, r, ((x + d) % nx) * 2 + lane, x_send.at[k, d])

    def d_copy(k, d):
        slot = ((r + k) % rows) * cols + ((x + d) % nx) * 2 + lane
        return push(slot, r, sibling, d_send.at[k, d])

    def arrived(slot):
        push(slot, r, sibling, d_send.at[0, 0]).wait_recv()

    def spread(k):
        for d in range(1, nx):
            x_copy(k, d).start()
        d_copy(k, 0).start()

    for k in range(1, rows):
        z_copy(k).start()
    spread(0)

    def halo_copies(phase, first, times):
        span = pl.ds(first, times)
        jobs = []
        for n, (src, dst, dr) in enumerate([(tile_rows, 0, 1), (1, tile_rows + 1, -1)]):
            jobs.append((xp.at[span, src], xp.at[span, dst], dr, 0, n))
        for side, dc in ((0, 1), (1, -1)):
            for dr in (-1, 0, 1):
                jobs.append((col_out.at[span, side], col_in.at[span, side, 1 - dr], dr, dc, 2 + side * 3 + dr + 1))
        made = []
        for src, dst, dr, dc, n in jobs:
            to_row, to_col, from_row, from_col = r + dr, c + dc, r - dr, c - dc
            sends = (to_row >= 0) & (to_row < rows) & (to_col >= 0) & (to_col < cols)
            gets = (from_row >= 0) & (from_row < rows) & (from_col >= 0) & (from_col < cols)
            copy = pltpu.make_async_remote_copy(
                src_ref=src, dst_ref=dst, send_sem=halo_send.at[phase, n], recv_sem=halo_recv.at[phase, n],
                device_id=(v, lax.select(sends, to_row, r), lax.select(sends, to_col, c)), device_id_type=MESH,
            )
            made.append((copy, dst, sends, gets))
        return made

    def place(t, load_row):
        pad_low = jnp.zeros((1, channels), F32)
        pad_high = jnp.zeros((PITCH - tile_cols - 1, channels), F32)
        for q in range(tile_rows):
            xp[t, q + 1] = jnp.concatenate([pad_low, load_row(q), pad_high], axis=0).astype(BF16)

    def set_columns(t, ends):
        blank = jnp.zeros((tile_rows, channels), F32)
        for side, column in enumerate(ends):
            col_out[t, side] = jnp.concatenate([column, blank], axis=0).astype(BF16)

    def send_halo(copies):
        for copy, dst, sends, gets in copies:
            pl.when(sends)(copy.start)

            @pl.when(jnp.logical_not(gets))
            def _(dst=dst):
                dst[...] = jnp.zeros(dst.shape, BF16)

    def take_halo(copies):
        for copy, dst, sends, gets in copies:
            pl.when(gets)(copy.wait_recv)
            pl.when(sends)(copy.wait_send)

    def insert_columns(t):
        at = lax.broadcasted_iota(jnp.int32, (PITCH, channels), 0)
        ends = []
        for side in range(2):
            above, beside, below = (col_in[t, side, n].astype(F32) for n in range(3))
            ends.append(
                [above[tile_rows - 1 : tile_rows]] + [beside[q : q + 1] for q in range(tile_rows)] + [below[:1]]
            )
        for q in range(tile_rows + 2):
            row = xp[t, q].astype(F32)
            row = jnp.where(at == 0, ends[0][q], jnp.where(at == tile_cols + 1, ends[1][q], row))
            xp[t, q] = row.astype(BF16)

    def convolve(t, fresh):
        lines = [xp[t, i : i + tile_rows].reshape(tile_rows * PITCH, channels) for i in range(3)]
        for j in range(3):
            part = sum(jnp.dot(lines[i], wc[t, i, j], preferred_element_type=F32) for i in range(3))
            if fresh:
                sums[j] = part
            else:
                sums[j] += part

    loads[0].wait()
    for t in range(2):
        place(t, lambda q: cache[t, q].astype(F32))
        tile = [cache[t, q].astype(F32) for q in range(tile_rows)]
        set_columns(
            t,
            [
                jnp.concatenate([line[tile_cols - 1 :] for line in tile], axis=0),
                jnp.concatenate([line[:1] for line in tile], axis=0),
            ],
        )
    cache_halo = halo_copies(0, 0, 2)
    send_halo(cache_halo)

    loads[1].wait()
    loads[2].wait()
    query = (jnp.dot(normed, wq[...], preferred_element_type=F32) * (1.0 / math.sqrt(channels))).astype(BF16)
    qk[...] = lax.dot_general(query, wk[...], (((1,), (1,)), ((), ())), preferred_element_type=F32).astype(BF16)
    peak[...] = jnp.full(peak.shape, -1e30, F32)
    total[...] = jnp.zeros(total.shape, F32)
    acc[...] = jnp.zeros(acc.shape, F32)

    take_halo(cache_halo)
    loads[3].wait()
    for t in range(2):
        insert_columns(t)
        convolve(t, t == 0)

    def cross(k):
        for d in range(1, nx):
            arrived(((r + k) % rows) * cols + ((x + d) % nx) * 2 + lane)
            d_copy(k, d).start()

    def attend(k):
        row = (r + k) % rows
        for d in range(nx):
            arrived(row * cols + d * 2 + 1 - lane)
        keys = kv[pl.ds(row * cols, cols)].reshape(cols * count, channels)
        scores = lax.dot_general(qk[...], keys, (((1,), (1,)), ((), ())), preferred_element_type=F32)
        old = peak[:, :1]
        new = jnp.maximum(old, jnp.max(scores, axis=1, keepdims=True))
        weights = jnp.exp(scores - new)
        scale = jnp.exp(old - new)
        total[...] = jnp.broadcast_to(total[:, :1] * scale + jnp.sum(weights, axis=1, keepdims=True), total.shape)
        acc[...] = acc[...] * scale + jnp.dot(weights.astype(BF16), keys, preferred_element_type=F32)
        peak[...] = jnp.broadcast_to(new, peak.shape)

    @pl.loop(1, rows)
    def _(k):
        arrived(((r + k) % rows) * cols + c)
        spread(k)
        cross(k - 1)
        attend(k - 1)

    cross(rows - 1)
    attend(rows - 1)

    loads[4].wait()
    loads[5].wait()
    pooled = (acc[...] / total[:, :1]).astype(BF16)
    attended = jnp.dot(pooled, wv[...], preferred_element_type=F32).astype(BF16)
    hidden = (tok[...] + jnp.dot(attended, wo[...], preferred_element_type=F32)).astype(BF16)
    hidden32 = hidden.astype(F32)
    tok[...] = hidden32
    scaled = rms_scaled(hidden32, cgain_ref[...])
    acc[...] = scaled / (1.0 + jnp.exp(-scaled))
    place(2, lambda q: acc[pl.ds(q * tile_cols, tile_cols), :])
    set_columns(
        2, [
            jnp.concatenate([acc[pl.ds(q * tile_cols + e, 1), :] for q in range(tile_rows)], axis=0)
            for e in (tile_cols - 1, 0)
        ]
    )
    frame_halo = halo_copies(1, 2, 1)
    send_halo(frame_halo)
    for q in range(tile_rows):
        hidden_ref[q] = tok[pl.ds(q * tile_cols, tile_cols), :].astype(BF16)
    take_halo(frame_halo)
    insert_columns(2)
    convolve(2, False)
    for q in range(tile_rows):
        line = tok[pl.ds(q * tile_cols, tile_cols), :out_channels] + bias_ref[...]
        for j in range(3):
            line = line + sums[j, pl.ds(q * PITCH + j, tile_cols), :]
        mixed_ref[q] = line.astype(BF16)

    for k in range(1, rows):
        z_copy(k).wait_send()

    @pl.loop(0, rows)
    def _(k):
        for d in range(1, nx):
            x_copy(k, d).wait_send()
        for d in range(nx):
            d_copy(k, d).wait_send()


def solution(mesh):
    rows, cols = mesh.shape["rows"], mesh.shape["cols"]

    def body(frame_in, norm_gain, w_query, w_key, w_value, w_out, conv_gain, conv_cache, w_conv, conv_bias):
        tile_rows, tile_cols, channels = frame_in.shape
        out_channels = w_conv.shape[-1]
        count = tile_rows * tile_cols
        wide = tile_rows * PITCH
        vmem, held = pl.BlockSpec(memory_space=pltpu.VMEM), pl.BlockSpec(memory_space=pl.ANY)
        dma = pltpu.SemaphoreType.DMA
        square = pltpu.VMEM((channels, channels), BF16)
        return pl.pallas_call(
            functools.partial(kernel, rows, cols),
            out_shape=(
                jax.ShapeDtypeStruct(frame_in.shape, BF16),
                jax.ShapeDtypeStruct((tile_rows, tile_cols, out_channels), BF16),
            ),
            in_specs=[vmem, vmem, held, held, held, held, vmem, held, held, vmem],
            out_specs=(vmem, vmem),
            scratch_shapes=[
                square, square, square, square,
                pltpu.VMEM(w_conv.shape, BF16),
                pltpu.VMEM(conv_cache.shape, BF16),
                pltpu.VMEM((rows * cols, count, channels), BF16),
                pltpu.VMEM((count, channels), F32),
                pltpu.VMEM((count, channels), BF16),
                pltpu.VMEM((count, channels), F32),
                pltpu.VMEM((count, 128), F32),
                pltpu.VMEM((count, 128), F32),
                pltpu.VMEM((3, tile_rows + 2, PITCH, channels), BF16),
                pltpu.VMEM((3, 2, 2 * tile_rows, channels), BF16),
                pltpu.VMEM((3, 2, 3, 2 * tile_rows, channels), BF16),
                pltpu.VMEM((3, wide, out_channels), F32),
                dma((6,)), dma((rows,)), dma((rows, cols // 2)), dma((rows, cols // 2)), dma((rows * cols,)),
                dma((2, 8)), dma((2, 8)),
            ],
            compiler_params=pltpu.CompilerParams(
                collective_id=0, has_side_effects=True, vmem_limit_bytes=56 * 1024 * 1024
            ),
        )(
            frame_in, norm_gain.reshape(1, channels), w_query, w_key, w_value, w_out,
            conv_gain.reshape(1, channels), conv_cache, w_conv, conv_bias.reshape(1, out_channels),
        )

    tiles = P(("video", "rows"), "cols", None)
    in_specs = (tiles, P(), P(), P(), P(), P(), P(), P(None, ("video", "rows"), "cols", None), P(), P())
    return jax.shard_map(body, mesh=mesh, in_specs=in_specs, out_specs=(tiles, tiles), check_vma=False)
```

time: 102 us -> 54.1 us (0.53)
  Pallas kernels: 0 us -> 46.4 us
  local copies, waits for them, and re-layouts: 34.8 us -> 6.64 us
  starting transfers between devices: 22.2 us -> 0 us
  matrix products: 14.7 us -> 0 us
  between operations: 14.7 us -> 0.64 us
  waiting for transfers between devices: 8.92 us -> 0 us
  other arithmetic: 5.83 us -> 0 us
    pallas_call x0 -> x1, Pallas kernels: none -> 46.4 us  [body(): pl.pallas_call(functools.partial(kernel, rows, cols), out_shape=(jax.Shap...]
    ppermute x8 -> x0, starting transfers between devices: 22.2 us -> none  [the longest x4 13.1 us: padded_2(): before = lax.ppermute(last, axis, up)]
    unnamed x41 -> x2, local copies, waits for them, and re-layouts: 22.5 us -> 3.45 us
    dot_general x5 -> x0, matrix products: 14.7 us -> none  [the longest x1 5.69 us: body(): jnp.dot(patches, kernel_rows, preferred_element_type=jnp.float32)]
    slice x23 -> x0, local copies, waits for them, and re-layouts: 7.18 us -> none  [the longest x20 5.92 us: body(): padded[time_off, row_off:row_off + tile_rows, col_off:col_off + tile_cols...]
    all_gather x1 -> x0, waiting for transfers between devices: 5.64 us -> none  [body(): lax.all_gather(normed, ('rows', 'cols'), axis=0, tiled=True)]
    concatenate x29 -> x0, local copies, waits for them, and re-layouts: 3.75 us -> none  [the longest x27 3.61 us: body(): patches = jnp.concatenate(windows, axis=-1).reshape(count, 27 * channels)]
    ppermute x8 -> x0, waiting for transfers between devices: 3.27 us -> none  [the longest x4 3.26 us: padded_2(): after = lax.ppermute(first, axis, down)]
  transfers between devices with their start and end apart: 9 -> 0, of which waited for: 2 -> 0; matrix products, arithmetic and copies ran while one was open for 30% -> 0% of each run, Pallas kernels for 0% -> 0%
where the time goes in v1:
time: 54.1 us; the launch traced here: 53.7 us
  Pallas kernels  46.4 us (86%)
  local copies, waits for them, and re-layouts  6.64 us (12%)
  between operations  0.64 us (1%)
    pallas_call x1, Pallas kernels, body(): pl.pallas_call(functools.partial(kernel, rows, cols), out_shape=(jax.Shap...  46.4 us
    unnamed x2, local copies, waits for them, and re-layouts  3.45 us
    pallas_call x2, local copies, waits for them, and re-layouts, body(): pl.pallas_call(functools.partial(kernel, rows, cols), out_shape=(jax.Shap...  3.19 us

profile of v1, /device:TPU:1, one launch (start us, length us, event | category | flops | bytes accessed | tf_op | source)
XLA Modules:
  0.0 53.7 jit_solution(3422804085492610663)
XLA Ops:
  0.6 1.6 %copy.12.frame_ref = bf16[8,20,512]{2,1,0:T(8,128)(2,1)} copy(bf16[8,20,512]{2,0,1:T(8,128)(2,1)} %param.10) | data formatting | bytes 327680 | tf_op args[0]
  2.3 1.8 %copy.13.cache_hbm = bf16[2,8,20,512]{3,2,1,0:T(8,128)(2,1)} copy(bf16[2,8,20,512]{3,1,2,0:T(8,128)(2,1)} %param.17) | data formatting | bytes 655360 | tf_op args[7]
  4.1 46.4 %shard_map.113 = (bf16[8,20,512]{2,1,0:T(8,128)(2,1)}, bf16[8,20,256]{2,1,0:T(8,128)(2,1)}) custom-call(bf16[8,20,512]{2,1,0:T(8,128)(2,1)} %copy.12.frame_ref, f32[1,512]{1,0:T(1,128)} %bitcast.3, bf16[512,512]{1,0:T(8,128)(2,1)} %wq_hbm.1, bf16[512,512]{1,0:T(8,128)(2,1)} %wk_hbm.1, bf16[512,512]{1,0:T(8,128)(2,1)} %wv_hbm.1, bf16[512,512]{1,0:T(8,128)(2,1)} %wo_hbm.1, ...), custom_call_target="tpu_custom_call" | custom-call | tf_op jit(solution)/shard_map/pallas_call | solution.py:264
  50.5 1.6 %copy.14 = bf16[8,20,512]{2,0,1:T(8,128)(2,1)} copy(bf16[8,20,512]{2,1,0:T(8,128)(2,1)} %get-tuple-element.2) | data formatting | bytes 327680 | tf_op jit(solution)/shard_map/pallas_call | solution.py:264
  52.1 1.5 %copy.15 = bf16[8,20,256]{2,0,1:T(8,128)(2,1)} copy(bf16[8,20,256]{2,1,0:T(8,128)(2,1)} %get-tuple-element.3) | data formatting | bytes 163840 | tf_op jit(solution)/shard_map/pallas_call | solution.py:264

commit v2 on v1

--- a/solution.py
+++ b/solution.py
@@ -11,7 +11,6 @@
 MESH = pl.DeviceIdType.MESH
 F32 = jnp.float32
 BF16 = jnp.bfloat16
-PITCH = 32
 
 
 def rms_scaled(values, gain):
@@ -22,10 +21,10 @@
 def kernel(
     rows, cols, frame_ref, ngain_ref, wq_hbm, wk_hbm, wv_hbm, wo_hbm, cgain_ref, cache_hbm, wc_hbm, bias_ref,
     hidden_ref, mixed_ref,
-    wq, wk, wv, wo, wc, cache, kv, tok, qk, acc, peak, total, xp, col_out, col_in, sums,
+    wq, wk, wv, wo, wc, cache, kv, tok, qk, acc, peak, total, pad, flat, row_out, row_in, col_in, even, odd, sums,
     load_sem, z_send, x_send, d_send, recv_sem, halo_send, halo_recv,
 ):
-    tile_rows, tile_cols, channels = frame_ref.shape
+    tile_cols, tile_rows, channels = frame_ref.shape
     out_channels = wc.shape[-1]
     count = tile_rows * tile_cols
     v, r, c = lax.axis_index("video"), lax.axis_index("rows"), lax.axis_index("cols")
@@ -33,6 +32,7 @@
     x, lane = c // 2, c % 2
     sibling = x * 2 + 1 - lane
     me = r * cols + c
+    parts = [(n, slice(n * 128, n * 128 + 128)) for n in range(channels // 128)]
 
     loads = [
         pltpu.make_async_copy(src, dst, load_sem.at[n])
@@ -51,8 +51,7 @@
         def _():
             pl.semaphore_signal(barrier, inc=1, device_id=(v, d // cols, d % cols), device_id_type=MESH)
 
-    for q in range(tile_rows):
-        tok[pl.ds(q * tile_cols, tile_cols), :] = frame_ref[q].astype(F32)
+    tok[...] = frame_ref[...].astype(F32).reshape(count, channels)
     normed = rms_scaled(tok[...], ngain_ref[...]).astype(BF16)
     kv[me] = normed
 
@@ -90,11 +89,12 @@
     def halo_copies(phase, first, times):
         span = pl.ds(first, times)
         jobs = []
-        for n, (src, dst, dr) in enumerate([(tile_rows, 0, 1), (1, tile_rows + 1, -1)]):
-            jobs.append((xp.at[span, src], xp.at[span, dst], dr, 0, n))
+        for side, dr in ((0, 1), (1, -1)):
+            jobs.append((row_out.at[span, side], row_in.at[span, side], dr, 0, side))
         for side, dc in ((0, 1), (1, -1)):
+            edge = pl.ds(count - 16 if side == 0 else 0, 16)
             for dr in (-1, 0, 1):
-                jobs.append((col_out.at[span, side], col_in.at[span, side, 1 - dr], dr, dc, 2 + side * 3 + dr + 1))
+                jobs.append((flat.at[span, edge], col_in.at[span, side, 1 - dr], dr, dc, 3 + side * 3 + dr))
         made = []
         for src, dst, dr, dc, n in jobs:
             to_row, to_col, from_row, from_col = r + dr, c + dc, r - dr, c - dc
@@ -107,16 +107,15 @@
             made.append((copy, dst, sends, gets))
         return made
 
-    def place(t, load_row):
-        pad_low = jnp.zeros((1, channels), F32)
-        pad_high = jnp.zeros((PITCH - tile_cols - 1, channels), F32)
-        for q in range(tile_rows):
-            xp[t, q + 1] = jnp.concatenate([pad_low, load_row(q), pad_high], axis=0).astype(BF16)
-
-    def set_columns(t, ends):
-        blank = jnp.zeros((tile_rows, channels), F32)
-        for side, column in enumerate(ends):
-            col_out[t, side] = jnp.concatenate([column, blank], axis=0).astype(BF16)
+    def place(t, values):
+        flat[t] = values.astype(BF16)
+        blank = jnp.zeros((row_out.shape[2] - tile_cols, 128), F32)
+        for n, lanes in parts:
+            for q in range(tile_cols):
+                pad[t, n, pl.ds((q + 1) * 16 + 8, 8), :] = values[q * 8 : q * 8 + 8, lanes]
+            for side, at in ((0, 15), (1, 8)):
+                line = pad[t, n, pl.ds(16 + at, tile_cols, stride=16), :]
+                row_out[t, side, :, lanes] = jnp.concatenate([line, blank], axis=0).astype(BF16)
 
     def send_halo(copies):
         for copy, dst, sends, gets in copies:
@@ -129,41 +128,41 @@
     def take_halo(copies):
         for copy, dst, sends, gets in copies:
             pl.when(gets)(copy.wait_recv)
+
+    def end_halo(copies):
+        for copy, dst, sends, gets in copies:
             pl.when(sends)(copy.wait_send)
 
-    def insert_columns(t):
-        at = lax.broadcasted_iota(jnp.int32, (PITCH, channels), 0)
-        ends = []
-        for side in range(2):
-            above, beside, below = (col_in[t, side, n].astype(F32) for n in range(3))
-            ends.append(
-                [above[tile_rows - 1 : tile_rows]] + [beside[q : q + 1] for q in range(tile_rows)] + [below[:1]]
-            )
-        for q in range(tile_rows + 2):
-            row = xp[t, q].astype(F32)
-            row = jnp.where(at == 0, ends[0][q], jnp.where(at == tile_cols + 1, ends[1][q], row))
-            xp[t, q] = row.astype(BF16)
-
-    def convolve(t, fresh):
-        lines = [xp[t, i : i + tile_rows].reshape(tile_rows * PITCH, channels) for i in range(3)]
-        for j in range(3):
-            part = sum(jnp.dot(lines[i], wc[t, i, j], preferred_element_type=F32) for i in range(3))
-            if fresh:
-                sums[j] = part
-            else:
-                sums[j] += part
+    def insert_halo(t):
+        for n, lanes in parts:
+            for side, (col, base) in enumerate(((0, 8), (tile_cols + 1, 0))):
+                above, beside, below = (col_in[t, side, near, :, lanes].astype(F32) for near in range(3))
+                pad[t, n, pl.ds(col * 16 + 8, 8), :] = beside[base : base + 8]
+                pad[t, n, pl.ds(col * 16 + 7, 1), :] = above[base + 7 : base + 8]
+                pad[t, n, pl.ds(col * 16 + 16, 1), :] = below[base : base + 1]
+            for side, at in ((0, 7), (1, 16)):
+                pad[t, n, pl.ds(16 + at, tile_cols, stride=16), :] = row_in[t, side, :, lanes].astype(F32)[:tile_cols]
+            for i in range(3):
+                lines = [pad[t, n, pl.ds(q * 16 + 7 + i, 8), :] for q in range(tile_cols + 2)]
+                for m in range(tile_cols // 2 + 1):
+                    both = jnp.concatenate(lines[2 * m : 2 * m + 2], axis=0)
+                    even[t, i, pl.ds(m * 16, 16), lanes] = both.astype(BF16)
+                for m in range(tile_cols // 2):
+                    both = jnp.concatenate(lines[2 * m + 1 : 2 * m + 3], axis=0)
+                    odd[t, i, pl.ds(m * 16, 16), lanes] = both.astype(BF16)
+
+    def convolve(t):
+        result = None
+        for i in range(3):
+            for j in range(3):
+                window = odd[t, i] if j == 1 else even[t, i, pl.ds(j * 8, count), :]
+                part = jnp.dot(window, wc[t, i, j], preferred_element_type=F32)
+                result = part if result is None else result + part
+        return result
 
     loads[0].wait()
     for t in range(2):
-        place(t, lambda q: cache[t, q].astype(F32))
-        tile = [cache[t, q].astype(F32) for q in range(tile_rows)]
-        set_columns(
-            t,
-            [
-                jnp.concatenate([line[tile_cols - 1 :] for line in tile], axis=0),
-                jnp.concatenate([line[:1] for line in tile], axis=0),
-            ],
-        )
+        place(t, cache[t].astype(F32).reshape(count, channels))
     cache_halo = halo_copies(0, 0, 2)
     send_halo(cache_halo)
 
@@ -177,9 +176,9 @@
 
     take_halo(cache_halo)
     loads[3].wait()
-    for t in range(2):
-        insert_columns(t)
-        convolve(t, t == 0)
+    insert_halo(0)
+    insert_halo(1)
+    sums[...] = convolve(0) + convolve(1)
 
     def cross(k):
         for d in range(1, nx):
@@ -216,29 +215,18 @@
     attended = jnp.dot(pooled, wv[...], preferred_element_type=F32).astype(BF16)
     hidden = (tok[...] + jnp.dot(attended, wo[...], preferred_element_type=F32)).astype(BF16)
     hidden32 = hidden.astype(F32)
-    tok[...] = hidden32
     scaled = rms_scaled(hidden32, cgain_ref[...])
-    acc[...] = scaled / (1.0 + jnp.exp(-scaled))
-    place(2, lambda q: acc[pl.ds(q * tile_cols, tile_cols), :])
-    set_columns(
-        2, [
-            jnp.concatenate([acc[pl.ds(q * tile_cols + e, 1), :] for q in range(tile_rows)], axis=0)
-            for e in (tile_cols - 1, 0)
-        ]
-    )
+    place(2, scaled / (1.0 + jnp.exp(-scaled)))
     frame_halo = halo_copies(1, 2, 1)
     send_halo(frame_halo)
-    for q in range(tile_rows):
-        hidden_ref[q] = tok[pl.ds(q * tile_cols, tile_cols), :].astype(BF16)
+    hidden_ref[...] = hidden32.reshape(hidden_ref.shape).astype(BF16)
+    sums[...] += hidden32[:, :out_channels] + bias_ref[...]
     take_halo(frame_halo)
-    insert_columns(2)
-    convolve(2, False)
-    for q in range(tile_rows):
-        line = tok[pl.ds(q * tile_cols, tile_cols), :out_channels] + bias_ref[...]
-        for j in range(3):
-            line = line + sums[j, pl.ds(q * PITCH + j, tile_cols), :]
-        mixed_ref[q] = line.astype(BF16)
-
+    insert_halo(2)
+    mixed_ref[...] = (sums[...] + convolve(2)).reshape(mixed_ref.shape).astype(BF16)
+
+    end_halo(cache_halo)
+    end_halo(frame_halo)
     for k in range(1, rows):
         z_copy(k).wait_send()
 
@@ -257,15 +245,17 @@
         tile_rows, tile_cols, channels = frame_in.shape
         out_channels = w_conv.shape[-1]
         count = tile_rows * tile_cols
-        wide = tile_rows * PITCH
+        edge = -(-tile_cols // 16) * 16
+        frame_in = frame_in.transpose(1, 0, 2)
+        conv_cache = conv_cache.transpose(0, 2, 1, 3)
         vmem, held = pl.BlockSpec(memory_space=pltpu.VMEM), pl.BlockSpec(memory_space=pl.ANY)
         dma = pltpu.SemaphoreType.DMA
         square = pltpu.VMEM((channels, channels), BF16)
-        return pl.pallas_call(
+        hidden, mixed_out = pl.pallas_call(
             functools.partial(kernel, rows, cols),
             out_shape=(
                 jax.ShapeDtypeStruct(frame_in.shape, BF16),
-                jax.ShapeDtypeStruct((tile_rows, tile_cols, out_channels), BF16),
+                jax.ShapeDtypeStruct((tile_cols, tile_rows, out_channels), BF16),
             ),
             in_specs=[vmem, vmem, held, held, held, held, vmem, held, held, vmem],
             out_specs=(vmem, vmem),
@@ -279,10 +269,14 @@
                 pltpu.VMEM((count, channels), F32),
                 pltpu.VMEM((count, 128), F32),
                 pltpu.VMEM((count, 128), F32),
-                pltpu.VMEM((3, tile_rows + 2, PITCH, channels), BF16),
-                pltpu.VMEM((3, 2, 2 * tile_rows, channels), BF16),
-                pltpu.VMEM((3, 2, 3, 2 * tile_rows, channels), BF16),
-                pltpu.VMEM((3, wide, out_channels), F32),
+                pltpu.VMEM((3, channels // 128, (tile_cols + 3) * 16, 128), F32),
+                pltpu.VMEM((3, count, channels), BF16),
+                pltpu.VMEM((3, 2, edge, channels), BF16),
+                pltpu.VMEM((3, 2, edge, channels), BF16),
+                pltpu.VMEM((3, 2, 3, 16, channels), BF16),
+                pltpu.VMEM((3, 3, count + 16, channels), BF16),
+                pltpu.VMEM((3, 3, count, channels), BF16),
+                pltpu.VMEM((count, out_channels), F32),
                 dma((6,)), dma((rows,)), dma((rows, cols // 2)), dma((rows, cols // 2)), dma((rows * cols,)),
                 dma((2, 8)), dma((2, 8)),
             ],
@@ -293,6 +287,7 @@
             frame_in, norm_gain.reshape(1, channels), w_query, w_key, w_value, w_out,
             conv_gain.reshape(1, channels), conv_cache, w_conv, conv_bias.reshape(1, out_channels),
         )
+        return hidden.transpose(1, 0, 2), mixed_out.transpose(1, 0, 2)
 
     tiles = P(("video", "rows"), "cols", None)
     in_specs = (tiles, P(), P(), P(), P(), P(), P(), P(None, ("video", "rows"), "cols", None), P(), P())

time: 54.1 us -> 50.5 us (0.933)
  local copies, waits for them, and re-layouts: 6.64 us -> 3.12 us
    pallas_call x2 -> x0, local copies, waits for them, and re-layouts: 3.19 us -> none  [body(): pl.pallas_call(functools.partial(kernel, rows, cols), out_shape=(jax.Shap...]
where the time goes in v2:
time: 50.5 us; the launch traced here: 50.1 us
  Pallas kernels  46.3 us (92%)
  local copies, waits for them, and re-layouts  3.12 us (6%)
  between operations  0.64 us (1%)
    pallas_call x1, Pallas kernels, body(): pl.pallas_call(functools.partial(kernel, rows, cols), out_shape=(jax.Shap...  46.3 us
    unnamed x2, local copies, waits for them, and re-layouts  3.12 us

profile of v2, /device:TPU:1, one launch (start us, length us, event | category | flops | bytes accessed | tf_op | source)
XLA Modules:
  0.0 50.1 jit_solution(3581873718452017311)
XLA Ops:
  0.6 46.3 %shard_map.113 = (bf16[20,8,512]{2,1,0:T(8,128)(2,1)}, bf16[20,8,256]{2,1,0:T(8,128)(2,1)}) custom-call(bf16[20,8,512]{2,1,0:T(8,128)(2,1)} %bitcast.9, f32[1,512]{1,0:T(1,128)} %bitcast.11, bf16[512,512]{1,0:T(8,128)(2,1)} %wq_hbm.1, bf16[512,512]{1,0:T(8,128)(2,1)} %wk_hbm.1, bf16[512,512]{1,0:T(8,128)(2,1)} %wv_hbm.1, bf16[512,512]{1,0:T(8,128)(2,1)} %wo_hbm.1, ...), custom_call_target="tpu_custom_call" | custom-call | tf_op jit(solution)/shard_map/pallas_call | solution.py:254
  46.9 1.6 %copy.14 = bf16[8,20,512]{2,0,1:T(8,128)(2,1)} copy(bf16[8,20,512]{2,0,1:T(8,128)(2,1)} %bitcast.8) | data formatting | bytes 327680
  48.5 1.5 %copy.15 = bf16[8,20,256]{2,0,1:T(8,128)(2,1)} copy(bf16[8,20,256]{2,0,1:T(8,128)(2,1)} %bitcast.10) | data formatting | bytes 163840

commit v3 on v2

--- a/solution.py
+++ b/solution.py
@@ -45,46 +45,61 @@
 
     barrier = pltpu.get_barrier_semaphore()
 
-    @pl.loop(0, rows * cols)
-    def _(d):
-        @pl.when(d != me)
-        def _():
-            pl.semaphore_signal(barrier, inc=1, device_id=(v, d // cols, d % cols), device_id_type=MESH)
+    near = [(r + dr, c + dc) for dr in (-1, 0, 1) for dc in (-1, 0, 1) if dr or dc]
+    peers = [((row >= 0) & (row < rows) & (col >= 0) & (col < cols), row, col) for row, col in near]
+    peers += [(None, r, ((x + d) % nx) * 2 + lane) for d in range(1, nx)]
+    for there, row, col in peers:
+
+        def greet(row=row, col=col):
+            pl.semaphore_signal(barrier, inc=1, device_id=(v, row, col), device_id_type=MESH)
+
+        greet() if there is None else pl.when(there)(greet)
 
     tok[...] = frame_ref[...].astype(F32).reshape(count, channels)
     normed = rms_scaled(tok[...], ngain_ref[...]).astype(BF16)
     kv[me] = normed
 
-    pl.semaphore_wait(barrier, rows * cols - 1)
-
-    def push(slot, row, col, send_sem):
+    tall = 1 + (r > 0).astype(jnp.int32) + (r + 1 < rows).astype(jnp.int32)
+    broad = 1 + (c > 0).astype(jnp.int32) + (c + 1 < cols).astype(jnp.int32)
+    pl.semaphore_wait(barrier, tall * broad - 1 + nx - 1)
+
+    half = count // 2
+
+    def push(slot, h, row, col, send_sem):
+        piece = kv.at[slot, pl.ds(h * half, half)]
         return pltpu.make_async_remote_copy(
-            src_ref=kv.at[slot], dst_ref=kv.at[slot], send_sem=send_sem, recv_sem=recv_sem.at[slot],
+            src_ref=piece, dst_ref=piece, send_sem=send_sem, recv_sem=recv_sem.at[slot, h],
             device_id=(v, row, col), device_id_type=MESH,
         )
 
-    def z_copy(k):
-        return push(me, (r + rows - k) % rows, c, z_send.at[k])
-
-    def x_copy(k, d):
-        slot = ((r + k) % rows) * cols + c
-        return push(slot, r, ((x + d) % nx) * 2 + lane, x_send.at[k, d])
-
-    def d_copy(k, d):
-        slot = ((r + k) % rows) * cols + ((x + d) % nx) * 2 + lane
-        return push(slot, r, sibling, d_send.at[k, d])
-
-    def arrived(slot):
-        push(slot, r, sibling, d_send.at[0, 0]).wait_recv()
-
-    def spread(k):
+    def z_copy(row, h, way):
+        return push(row * cols + c, h, r + (1 if way == 0 else -1), c, z_send.at[way, row, h])
+
+    def x_copy(row, h, d):
+        return push(row * cols + c, h, r, ((x + d) % nx) * 2 + lane, x_send.at[row, d, h])
+
+    def d_copy(row, h, d):
+        return push(row * cols + ((x + d) % nx) * 2 + lane, h, r, sibling, d_send.at[row, d, h])
+
+    def arrived(slot, h):
+        push(slot, h, r, sibling, d_send.at[0, 0, 0]).wait_recv()
+
+    def can_pass(way):
+        return r + 1 < rows if way == 0 else r > 0
+
+    def spread(row, h, ways):
+        for way in ways:
+            pl.when(can_pass(way))(lambda way=way: z_copy(row, h, way).start())
         for d in range(1, nx):
-            x_copy(k, d).start()
-        d_copy(k, 0).start()
-
-    for k in range(1, rows):
-        z_copy(k).start()
-    spread(0)
+            x_copy(row, h, d).start()
+        d_copy(row, h, 0).start()
+
+    def source(k, way):
+        row = r - k if way == 0 else r + k
+        return row, (row >= 0) & (row < rows)
+
+    for h in range(2):
+        spread(r, h, (0, 1))
 
     def halo_copies(phase, first, times):
         span = pl.ds(first, times)
@@ -174,21 +189,26 @@
     total[...] = jnp.zeros(total.shape, F32)
     acc[...] = jnp.zeros(acc.shape, F32)
 
-    take_halo(cache_halo)
-    loads[3].wait()
-    insert_halo(0)
-    insert_halo(1)
-    sums[...] = convolve(0) + convolve(1)
-
-    def cross(k):
+    def pass_on(k):
+        for way in range(2):
+            row, valid = source(k, way)
+
+            @pl.when(valid)
+            def _(row=row, way=way):
+                for h in range(2):
+                    arrived(row * cols + c, h)
+                    spread(row, h, (way,))
+
+    def cross(row):
         for d in range(1, nx):
-            arrived(((r + k) % rows) * cols + ((x + d) % nx) * 2 + lane)
-            d_copy(k, d).start()
-
-    def attend(k):
-        row = (r + k) % rows
+            for h in range(2):
+                arrived(row * cols + ((x + d) % nx) * 2 + lane, h)
+                d_copy(row, h, d).start()
+
+    def attend(row):
         for d in range(nx):
-            arrived(row * cols + d * 2 + 1 - lane)
+            for h in range(2):
+                arrived(row * cols + d * 2 + 1 - lane, h)
         keys = kv[pl.ds(row * cols, cols)].reshape(cols * count, channels)
         scores = lax.dot_general(qk[...], keys, (((1,), (1,)), ((), ())), preferred_element_type=F32)
         old = peak[:, :1]
@@ -199,15 +219,37 @@
         acc[...] = acc[...] * scale + jnp.dot(weights.astype(BF16), keys, preferred_element_type=F32)
         peak[...] = jnp.broadcast_to(new, peak.shape)
 
-    @pl.loop(1, rows)
+    def finish(k):
+        for way in range(2):
+            row, valid = source(k, way)
+
+            @pl.when(valid)
+            def _(row=row):
+                cross(row)
+                attend(row)
+
+    pass_on(1)
+    take_halo(cache_halo)
+    loads[3].wait()
+    insert_halo(0)
+    insert_halo(1)
+    sums[...] = convolve(0)
+    cross(r)
+    attend(r)
+
+    @pl.loop(2, rows)
     def _(k):
-        arrived(((r + k) % rows) * cols + c)
-        spread(k)
-        cross(k - 1)
-        attend(k - 1)
-
-    cross(rows - 1)
-    attend(rows - 1)
+        pass_on(k)
+
+        @pl.when(k == 2)
+        def _():
+            sums[...] += convolve(1)
+
+        finish(k - 1)
+
+    if rows <= 2:
+        sums[...] += convolve(1)
+    finish(rows - 1)
 
     loads[4].wait()
     loads[5].wait()
@@ -227,15 +269,19 @@
 
     end_halo(cache_halo)
     end_halo(frame_halo)
-    for k in range(1, rows):
-        z_copy(k).wait_send()
-
     @pl.loop(0, rows)
-    def _(k):
-        for d in range(1, nx):
-            x_copy(k, d).wait_send()
-        for d in range(nx):
-            d_copy(k, d).wait_send()
+    def _(row):
+        for h in range(2):
+            for way in range(2):
+
+                @pl.when(can_pass(way) & (row <= r if way == 0 else row >= r))
+                def _(h=h, way=way):
+                    z_copy(row, h, way).wait_send()
+
+            for d in range(1, nx):
+                x_copy(row, h, d).wait_send()
+            for d in range(nx):
+                d_copy(row, h, d).wait_send()
 
 
 def solution(mesh):
@@ -277,7 +323,7 @@
                 pltpu.VMEM((3, 3, count + 16, channels), BF16),
                 pltpu.VMEM((3, 3, count, channels), BF16),
                 pltpu.VMEM((count, out_channels), F32),
-                dma((6,)), dma((rows,)), dma((rows, cols // 2)), dma((rows, cols // 2)), dma((rows * cols,)),
+                dma((6,)), dma((2, rows, 2)), dma((rows, cols // 2, 2)), dma((rows, cols // 2, 2)), dma((rows * cols, 2)),
                 dma((2, 8)), dma((2, 8)),
             ],
             compiler_params=pltpu.CompilerParams(

time: 50.5 us -> 37.6 us (0.74)
  Pallas kernels: 46.3 us -> 33.7 us
    pallas_call x1, Pallas kernels: 46.3 us -> 33.7 us  [body(): pl.pallas_call(functools.partial(kernel, rows, cols), out_shape=(jax.Shap...]
where the time goes in v3:
time: 37.6 us; the launch traced here: 37.4 us
  Pallas kernels  33.7 us (90%)
  local copies, waits for them, and re-layouts  3.12 us (8%)
  between operations  0.64 us (2%)
    pallas_call x1, Pallas kernels, body(): pl.pallas_call(functools.partial(kernel, rows, cols), out_shape=(jax.Shap...  33.7 us
    unnamed x2, local copies, waits for them, and re-layouts  3.12 us

profile of v3, /device:TPU:1, one launch (start us, length us, event | category | flops | bytes accessed | tf_op | source)
XLA Modules:
  0.0 37.4 jit_solution(12358606267490995610)
XLA Ops:
  0.6 33.7 %shard_map.113 = (bf16[20,8,512]{2,1,0:T(8,128)(2,1)}, bf16[20,8,256]{2,1,0:T(8,128)(2,1)}) custom-call(bf16[20,8,512]{2,1,0:T(8,128)(2,1)} %bitcast.9, f32[1,512]{1,0:T(1,128)} %bitcast.11, bf16[512,512]{1,0:T(8,128)(2,1)} %wq_hbm.1, bf16[512,512]{1,0:T(8,128)(2,1)} %wk_hbm.1, bf16[512,512]{1,0:T(8,128)(2,1)} %wv_hbm.1, bf16[512,512]{1,0:T(8,128)(2,1)} %wo_hbm.1, ...), custom_call_target="tpu_custom_call" | custom-call | tf_op jit(solution)/shard_map/pallas_call | solution.py:300
  34.3 1.6 %copy.14 = bf16[8,20,512]{2,0,1:T(8,128)(2,1)} copy(bf16[8,20,512]{2,0,1:T(8,128)(2,1)} %bitcast.8) | data formatting | bytes 327680
  35.9 1.5 %copy.15 = bf16[8,20,256]{2,0,1:T(8,128)(2,1)} copy(bf16[8,20,256]{2,0,1:T(8,128)(2,1)} %bitcast.10) | data formatting | bytes 163840
